TPU v7x, 512 devices: a whole 4x8x8 slice. The times are simulated.
512 devices in a mesh: rep: 8 (over x, core), fsdp: 64 (over y, z).
Axes of the slice: x: 4, y: 8, z: 8, core: 2. Of those that a mesh axis runs over, the one named last changes fastest.
Arguments:
- partials: bfloat16 [8, 8, 30, 512, 512], P('rep', None, None, 'fsdp'), may hold values from -8 to 8
- momentum: float32 [8, 30, 512, 512], P('rep', None, 'fsdp'), may hold values from -6 to 6
- owners: int32 [8, 30], P('rep'), may hold values from 0 to 63, as said below
- factors: bfloat16 [8, 64, 2, 2, 512, 512], P('rep', 'fsdp'), may hold values from -4 to 4
Outputs:
- new_momentum: float32 [8, 30, 512, 512], P('rep', None, 'fsdp')
Inputs may be any that keep to these rules, and one draw needn't show every extreme that they name: `owners`: within each group, every index of fsdp owns at most 2 blocks, and one index owns exactly 2.
All inputs are finite; a program needn't handle non-finite values.
Results may differ from a plain program's by a relative error of at most 0.019.
Values may be sent and summed in bfloat16 or wider, within the bound.
A program may use at most 64 MiB of HBM per device.

v0:
```python
import jax
import jax.numpy as jnp
from jax import lax
from jax.sharding import PartitionSpec as P

EPSILON = 1e-06
BETA = 0.9


def slot_table(owned, nodes, slots):
    count = owned.shape[0]
    same = owned[:, None] == owned[None, :]
    earlier = lax.broadcasted_iota(jnp.int32, (count, count), 1) < lax.broadcasted_iota(
        jnp.int32, (count, count), 0
    )
    slot = jnp.sum((same & earlier).astype(jnp.int32), axis=1)
    target = owned * slots + slot
    places = lax.broadcasted_iota(jnp.int32, (nodes * slots, count), 0)
    return (places == target[None, :]).astype(jnp.bfloat16)


def precondition(blocks, held):
    left = jnp.einsum(
        "sij,sjk->sik", held[:, 0], blocks, preferred_element_type=jnp.float32
    ).astype(jnp.bfloat16)
    precond = jnp.einsum("sij,sjk->sik", left, held[:, 1], preferred_element_type=jnp.float32)
    grad_sq = jnp.sum(jnp.square(blocks.astype(jnp.float32)), axis=(1, 2))
    prec_sq = jnp.sum(precond * precond, axis=(1, 2))
    ratio = jnp.sqrt(grad_sq / (prec_sq + EPSILON))
    return (precond * ratio[:, None, None]).astype(jnp.bfloat16)


def local(partials, momentum, owners, factors):
    nodes = lax.axis_size("fsdp")
    slots = factors.shape[2]
    count = owners.shape[1]
    rows = partials.shape[3]
    width = partials.shape[4]
    summed = lax.psum_scatter(partials, "rep", scatter_dimension=1, tiled=True).astype(jnp.float32)
    grad = summed[0, 0].astype(jnp.bfloat16)
    select = slot_table(owners[0], nodes, slots)
    outgoing = jnp.dot(
        select, grad.reshape(count, rows * width), preferred_element_type=jnp.float32
    )
    outgoing = outgoing.astype(jnp.bfloat16).reshape(nodes, slots, rows, width)
    arrived = lax.all_to_all(outgoing, "fsdp", split_axis=0, concat_axis=2, tiled=True)
    update = precondition(arrived[0], factors[0, 0])
    returned = lax.all_to_all(update[None], "fsdp", split_axis=2, concat_axis=0, tiled=True)
    gathered = jnp.einsum(
        "pb,pk->bk",
        select,
        returned.reshape(nodes * slots, rows * width),
        preferred_element_type=jnp.float32,
    )
    return BETA * momentum + gathered.reshape(momentum.shape)


def solution(mesh):
    placed = (
        P("rep", None, None, "fsdp", None),
        P("rep", None, "fsdp", None),
        P("rep", None),
        P("rep", "fsdp", None, None, None, None),
    )
    return jax.shard_map(
        local, mesh=mesh, in_specs=placed, out_specs=P("rep", None, "fsdp", None), check_vma=False
    )
```

profile of v0, /device:TPU:22, one launch (start us, length us, event | category | flops | bytes accessed | tf_op | source)
XLA Modules:
  0.0 149.7 jit_solution(33286330874579465)
XLA Ops:
  6.5 0.0 reduce-scatter.2.cloned.1.call-start
  6.5 0.7 reduce-scatter.2.cloned.1.call-update
  7.3 0.9 convert_reduce_fusion
  8.2 0.7 fusion.12
  8.8 41.3 %reduce-scatter.2.cloned.1.call-done = bf16[1,1,30,8,512]{4,3,2,1,0:T(8,128)(2,1)} async-done(((bf16[1,8,30,8,512]{4,3,2,1,0:T(8,128)(2,1)}), bf16[1,1,30,8,512]{4,3,2,1,0:T(8,128)(2,1)}) %reduce-scatter.2.cloned.1.call-update) | async-done | bytes 245776 | tf_op jit(solution)/shard_map/reduce_scatter | solution.py:39
  50.1 1.0 pad
  51.1 0.1 copy.42
  51.2 0.5 convolution_convert_fusion
  51.8 0.0 copy-start
  51.8 1.4 copy.43
  53.1 13.4 %all-to-all-start = ((bf16[64,2,8,512]{3,2,1,0:T(8,128)(2,1)}), bf16[64,2,8,512]{3,2,1,0:T(8,128)(2,1)S(1)}, u32[]{:S(2)}, u32[]{:S(2)}) async-start(bf16[64,2,8,512]{3,2,1,0:T(8,128)(2,1)} %bitcast.24), calls=%async_computation.1 | async-start | bytes 2097152 | tf_op jit(solution)/shard_map/all_to_all | solution.py:46
  66.5 0.0 copy-done
  66.5 1.5 copy.55
  68.0 29.5 %all-to-all-done = bf16[64,2,8,512]{3,2,1,0:T(8,128)(2,1)S(1)} async-done(((bf16[64,2,8,512]{3,2,1,0:T(8,128)(2,1)}), bf16[64,2,8,512]{3,2,1,0:T(8,128)(2,1)S(1)}, u32[]{:S(2)}, u32[]{:S(2)}) %all-to-all-start) | async-done | bytes 1048608 | tf_op jit(solution)/shard_map/all_to_all | solution.py:46
  97.5 0.4 multiply_reduce_fusion.1
  97.9 3.1 %multiply_reduce_fusion = (f32[2]{0:T(128)S(1)}, f32[2,512,512]{2,1,0:T(8,128)S(1)}) fusion(bf16[2,2,512,512]{3,2,0,1:T(8,128)(2,1)} %bitcast.62, bf16[64,2,8,512]{3,2,1,0:T(8,128)(2,1)S(1)} %all-to-all-done), kind=kOutput, calls=%fused_computation.3 | convolution fusion | flops 1075314688 | bytes 5242888 | tf_op jit(solution)/shard_map/sij,sjk->sik/dot_general | solution.py:26
  101.0 0.3 fusion.1
  101.3 1.1 copy.36
  102.4 37.5 %all_to_all.30 = bf16[1,2,512,512]{3,1,0,2:T(2,128)(2,1)S(1)} all-to-all(bf16[1,2,512,512]{3,1,0,2:T(2,128)(2,1)S(1)} %copy.36), channel_id=1, replica_groups=mesh['rep'=8,'fsdp'=64] {'fsdp'}, dimensions={2} | all-to-all | bytes 2097152 | tf_op jit(solution)/shard_map/all_to_all | solution.py:48
  139.9 0.2 copy.37
  140.1 0.4 copy.44
  140.5 0.0 copy-start.1
  140.5 0.7 copy.38
  141.2 0.5 fusion.7
  141.7 0.0 copy-done.1
  141.7 1.1 bitcast_add_fusion
  (1 shorter events, 0.0 us)
Async XLA Ops:
  6.5 43.6 %reduce-scatter.2.cloned.1.call-start = ((), (), s32[]{:S(2)}) async-start(), calls=%async_computation.3 | async-start | bytes 2211840 | tf_op jit(solution)/shard_map/reduce_scatter | solution.py:39
  51.8 14.8 %copy-start = (bf16[1,1,2,2,512,512]{5,4,3,2,1,0:T(8,128)(2,1)S(1)}, bf16[1,1,2,2,512,512]{5,4,3,2,1,0:T(8,128)(2,1)}, u32[]{:S(2)}) copy-start(bf16[1,1,2,2,512,512]{5,4,3,2,1,0:T(8,128)(2,1)} %param.7) | copy-start | bytes 6291460
  53.1 44.3 %all-to-all-start = ((bf16[64,2,8,512]{3,2,1,0:T(8,128)(2,1)}), bf16[64,2,8,512]{3,2,1,0:T(8,128)(2,1)S(1)}, u32[]{:S(2)}, u32[]{:S(2)}) async-start(bf16[64,2,8,512]{3,2,1,0:T(8,128)(2,1)} %bitcast.24), calls=%async_computation.1 | async-start | bytes 2097152 | tf_op jit(solution)/shard_map/all_to_all | solution.py:46
  140.5 1.2 copy-start.1
Sparse Core Ops, SparseCore 0:
  10.2 39.8 reduce-scatter.1
where the time goes:
time: 150 us
  waiting for transfers between devices  71.5 us (48%)
  blocking collectives  37.5 us (25%)
  between operations  13.5 us (9%)
  starting transfers between devices  13.4 us (9%)
  local copies, waits for them, and re-layouts  6.3 us (4%)
  matrix products  4.1 us (3%)
  other arithmetic  3.44 us (2%)
    reduce_scatter x1, waiting for transfers between devices, local(): lax.psum_scatter(partials, 'rep', scatter_dimension=1, tiled=True)  41.3 us
    all_to_all x1, blocking collectives, local(): lax.all_to_all(update[None], 'fsdp', split_axis=2, concat_axis=0, tiled=T...  37.5 us
    all_to_all x1, waiting for transfers between devices, local(): lax.all_to_all(outgoing, 'fsdp', split_axis=0, concat_axis=2, tiled=True)  29.5 us
    all_to_all x1, starting transfers between devices, local(): lax.all_to_all(outgoing, 'fsdp', split_axis=0, concat_axis=2, tiled=True)  13.4 us
    unnamed x9, local copies, waits for them, and re-layouts  4.32 us
    dot_general x1, matrix products, precondition(): jnp.einsum('sij,sjk->sik', left, held[:, 1], preferred_element_type=jnp.f...  3.07 us
  transfers between devices with their start and end apart: 2, of which 2 were waited for; matrix products, arithmetic and copies ran while one was open for 2% of the time, Pallas kernels for 0%

commit v1 on v0

v1 whole, which is shorter than its diff:
```python
import functools

import jax
import jax.numpy as jnp
from jax import lax
from jax.experimental import pallas as pl
from jax.experimental.pallas import tpu as pltpu
from jax.sharding import PartitionSpec as P

EPSILON = 1e-06
BETA = 0.9
MESH = pl.DeviceIdType.MESH
F32 = jnp.float32
BF16 = jnp.bfloat16


def iota(shape, dim):
    return lax.broadcasted_iota(jnp.int32, shape, dim)


def kernel(
    nodes, count, rows, width, slots,
    owners, part, fac, out,
    sib, psum, own, xin, grad, pick_out, pick_in, held, out1, in1, left, prec, out2, in2,
    sib_send, sib_recv, x_send, x_recv, send1, recv1, send2, recv2, fac_sem,
):
    rep = lax.axis_index("rep")
    me = lax.axis_index("fsdp")
    chip, core = rep // 2, lax.rem(rep, 2)
    chips = part.shape[0]
    cols = width // 2
    quarter = width // 4
    lines = count * rows

    barrier = pltpu.get_barrier_semaphore()
    pl.semaphore_signal(
        barrier, inc=1, device_id={"rep": chip * 2 + 1 - core}, device_id_type=MESH
    )
    for k in range(1, chips):
        pl.semaphore_signal(
            barrier, inc=1, device_id={"rep": lax.rem(chip + k, chips) * 2 + core},
            device_id_type=MESH,
        )

    def greet(k, carry):
        pl.semaphore_signal(
            barrier, inc=1, device_id={"fsdp": lax.rem(me + k, nodes)}, device_id_type=MESH
        )
        return carry

    lax.fori_loop(1, nodes, greet, 0)
    pl.semaphore_wait(barrier, 1 + chips - 1 + nodes - 1)

    def to_sibling(h):
        return pltpu.make_async_remote_copy(
            src_ref=part.at[:, 1 - core, :, pl.ds(h * cols, cols)],
            dst_ref=sib.at[h],
            send_sem=sib_send.at[h],
            recv_sem=sib_recv.at[h],
            device_id={"rep": chip * 2 + 1 - core},
            device_id_type=MESH,
        )

    for h in range(2):
        to_sibling(h).start()
    load = pltpu.make_async_copy(fac, held, fac_sem)
    load.start()

    lane_block = iota((32, lines), 1) // rows
    sub = iota((32, lines), 0)
    own_lane = jnp.zeros((32, lines), jnp.int32)
    own_sub = jnp.full((32, lines), -1, jnp.int32)
    for b in range(count):
        own_lane = jnp.where(lane_block == b, owners[0, b], own_lane)
        own_sub = jnp.where(sub == b, owners[0, b], own_sub)
    earlier = (own_lane == own_sub) & (sub < lane_block)
    slot_lane = jnp.sum(earlier.astype(jnp.int32), axis=0, keepdims=True)
    place = own_lane[0:1] * rows + lax.rem(iota((1, lines), 1), rows)
    for s in range(slots):
        here = jnp.where(slot_lane == s, place, -1)
        match = iota((nodes * rows, lines), 0) == here
        pick_out[s] = jnp.where(match, 1.0, 0.0).astype(BF16)
    row_block = iota((lines, 128), 0) // rows
    lane = iota((lines, 128), 1)
    own_row = jnp.zeros((lines, 128), jnp.int32)
    own_other = jnp.full((lines, 128), -1, jnp.int32)
    for b in range(count):
        own_row = jnp.where(row_block == b, owners[0, b], own_row)
        own_other = jnp.where(lane == b, owners[0, b], own_other)
    earlier = (own_row == own_other) & (lane < row_block)
    slot_row = jnp.sum(earlier.astype(jnp.int32), axis=1, keepdims=True)
    place = own_row[:, 0:1] * rows + lax.rem(iota((lines, 1), 0), rows)
    for s in range(slots):
        here = jnp.where(slot_row == s, place, -1)
        match = iota((lines, nodes * rows), 1) == here
        pick_in[s] = jnp.where(match, 1.0, 0.0).astype(BF16)

    def to_chip(h, k):
        other = lax.rem(chip + k, chips)
        return pltpu.make_async_remote_copy(
            src_ref=psum.at[h, k - 1],
            dst_ref=xin.at[h, k - 1],
            send_sem=x_send.at[h],
            recv_sem=x_recv.at[h],
            device_id={"rep": other * 2 + core},
            device_id_type=MESH,
        )

    for h in range(2):
        side = pl.ds(h * cols, cols)
        to_sibling(h).wait_recv()
        for k in (2, 1, 3):
            other = lax.rem(chip + k, chips)
            mine = part[other, core, :, side].astype(F32)
            psum[h, k - 1] = (mine + sib[h, other].astype(F32)).astype(BF16)
            to_chip(h, k).start()
        own[h] = part[chip, core, :, side].astype(F32) + sib[h, chip].astype(F32)

    def send_loop(source, target, send, recv):
        def one(k, carry):
            p = lax.rem(me + k, nodes)
            pltpu.make_async_remote_copy(
                src_ref=source.at[p],
                dst_ref=target.at[me],
                send_sem=send,
                recv_sem=recv,
                device_id={"fsdp": p},
                device_id_type=MESH,
            ).start()
            return carry

        lax.fori_loop(1, nodes, one, 0)

    def bulk(source, target, send, recv):
        most = pl.ds(0, nodes - 1)
        return pltpu.make_async_remote_copy(
            src_ref=source.at[most],
            dst_ref=target.at[most],
            send_sem=send,
            recv_sem=recv,
            device_id={"fsdp": lax.rem(me + 1, nodes)},
            device_id_type=MESH,
        )

    def pack(s, h):
        step = 16

        def some(i, carry):
            which = pl.ds(pl.multiple_of(i * step * rows, step * rows), step * rows)
            picked = jnp.dot(pick_out[s, which, :], grad[h], preferred_element_type=F32)
            one = picked[:, :quarter].reshape(step, rows, quarter)
            two = picked[:, quarter:].reshape(step, rows, quarter)
            out1[s, h, pl.ds(i * step, step)] = jnp.concatenate([one, two], axis=1).astype(BF16)
            return carry

        lax.fori_loop(0, nodes // step, some, 0)
        in1[s, h, me] = out1[s, h, me]

    def send_grad(s, h):
        send_loop(out1.at[s, h], in1.at[s, h], send1.at[s, h], recv1.at[s, h])

    for h in range(2):
        pltpu.make_async_remote_copy(
            src_ref=psum.at[h], dst_ref=xin.at[h], send_sem=x_send.at[h], recv_sem=x_recv.at[h],
            device_id={"rep": chip * 2 + 1 - core}, device_id_type=MESH,
        ).wait_recv()
        total = own[h]
        for k in range(chips - 1):
            total = total + xin[h, k].astype(F32)
        grad[h] = total.astype(BF16)
        pack(0, h)
        send_grad(0, h)
        if h == 0:
            pack(1, 0)
    send_grad(1, 0)
    pack(1, 1)
    send_grad(1, 1)
    load.wait()

    for s in range(slots):
        grad_sq = jnp.zeros((1, 1), F32)
        for h in range(2):
            bulk(out1.at[s, h], in1.at[s, h], send1.at[s, h], recv1.at[s, h]).wait_recv()
            wide = in1[s, h].astype(F32)
            grad_sq = grad_sq + jnp.sum(wide * wide, keepdims=True).reshape(1, 1)
            one = wide[:, :rows].reshape(nodes * rows, quarter)
            two = wide[:, rows:].reshape(nodes * rows, quarter)
            block = jnp.concatenate([one, two], axis=1).astype(BF16)
            left[:, h * cols : (h + 1) * cols] = jnp.dot(
                held[s, 0], block, preferred_element_type=F32
            ).astype(BF16)
        prec[...] = jnp.dot(left[...], held[s, 1], preferred_element_type=F32)
        prec_sq = jnp.sum(prec[...] * prec[...], keepdims=True).reshape(1, 1)
        ratio = jnp.sqrt(grad_sq / (prec_sq + EPSILON))
        update = prec[...] * ratio
        one = update[:, :cols].reshape(nodes, rows, cols)
        two = update[:, cols:].reshape(nodes, rows, cols)
        out2[s] = jnp.concatenate([one, two], axis=1).astype(BF16)
        in2[s, me] = out2[s, me]
        send_loop(out2.at[s], in2.at[s], send2.at[s], recv2.at[s])

    for s in range(slots):
        bulk(out2.at[s], in2.at[s], send2.at[s], recv2.at[s]).wait_recv()
        wide = in2[s].astype(F32)
        for h in range(2):
            rows_h = wide[:, h * rows : (h + 1) * rows].reshape(nodes * rows, cols).astype(BF16)
            got = jnp.dot(pick_in[s], rows_h, preferred_element_type=F32)
            if s == 0:
                own[h] = got
            else:
                out[:, h * cols : (h + 1) * cols] = (own[h] + got).astype(BF16)

    for h in range(2):
        to_sibling(h).wait_send()
        pltpu.make_async_remote_copy(
            src_ref=psum.at[h], dst_ref=xin.at[h], send_sem=x_send.at[h], recv_sem=x_recv.at[h],
            device_id={"rep": chip * 2 + 1 - core}, device_id_type=MESH,
        ).wait_send()
    for s in range(slots):
        for h in range(2):
            bulk(out1.at[s, h], in1.at[s, h], send1.at[s, h], recv1.at[s, h]).wait_send()
        bulk(out2.at[s], in2.at[s], send2.at[s], recv2.at[s]).wait_send()


def local(partials, momentum, owners, factors):
    nodes = lax.axis_size("fsdp")
    slots = factors.shape[2]
    groups, count, rows, width = partials.shape[1:]
    lines = count * rows
    chips = groups // 2
    cols = width // 2
    vmem, dma = pltpu.VMEM, pltpu.SemaphoreType.DMA
    update = pl.pallas_call(
        functools.partial(kernel, nodes, count, rows, width, slots),
        out_shape=jax.ShapeDtypeStruct((lines, width), BF16),
        in_specs=[
            pl.BlockSpec(memory_space=pltpu.SMEM),
            pl.BlockSpec(memory_space=pltpu.VMEM),
            pl.BlockSpec(memory_space=pl.ANY),
        ],
        out_specs=pl.BlockSpec(memory_space=pltpu.VMEM),
        scratch_shapes=[
            vmem((2, chips, lines, cols), BF16),
            vmem((2, chips - 1, lines, cols), BF16),
            vmem((2, lines, cols), F32),
            vmem((2, chips - 1, lines, cols), BF16),
            vmem((2, lines, cols), BF16),
            vmem((slots, nodes * rows, lines), BF16),
            vmem((slots, lines, nodes * rows), BF16),
            vmem((slots, 2, width, width), BF16),
            vmem((slots, 2, nodes, 2 * rows, width // 4), BF16),
            vmem((slots, 2, nodes, 2 * rows, width // 4), BF16),
            vmem((width, width), BF16),
            vmem((width, width), F32),
            vmem((slots, nodes, 2 * rows, cols), BF16),
            vmem((slots, nodes, 2 * rows, cols), BF16),
            dma((2,)), dma((2,)), dma((2,)), dma((2,)),
            dma((slots, 2)), dma((slots, 2)), dma((slots,)), dma((slots,)),
            dma,
        ],
        compiler_params=pltpu.CompilerParams(
            collective_id=0, has_side_effects=True, vmem_limit_bytes=48 << 20
        ),
    )(owners, partials.reshape(chips, 2, lines, width), factors[0, 0])
    return BETA * momentum + update.astype(F32).reshape(momentum.shape)


def solution(mesh):
    placed = (
        P("rep", None, None, "fsdp", None),
        P("rep", None, "fsdp", None),
        P("rep", None),
        P("rep", "fsdp", None, None, None, None),
    )
    return jax.shard_map(
        local, mesh=mesh, in_specs=placed, out_specs=P("rep", None, "fsdp", None), check_vma=False
    )
```

time: 150 us -> 85.7 us (0.57)
  the two profiles are of different devices: /device:TPU:22 before, /device:TPU:1 now
where the time goes in v1:
time: 85.7 us; the launch traced here: 85.5 us
  Pallas kernels  80.9 us (94%)
  local copies, waits for them, and re-layouts  3.79 us (4%)
    pallas_call x1, Pallas kernels, local(): pl.pallas_call(functools.partial(kernel, nodes, count, rows, width, slots...  80.9 us
    unnamed x8, local copies, waits for them, and re-layouts  3.79 us

profile of v1, /device:TPU:1, one launch (start us, length us, event | category | flops | bytes accessed | tf_op | source)
XLA Modules:
  0.0 85.5 jit_solution(8944407729729120733)
XLA Ops:
  0.0 0.0 copy-start
  0.0 1.6 %copy-done = bf16[1,1,2,2,512,512]{5,4,3,2,1,0:T(8,128)(2,1)S(1)} copy-done((bf16[1,1,2,2,512,512]{5,4,3,2,1,0:T(8,128)(2,1)S(1)}, bf16[1,1,2,2,512,512]{5,4,3,2,1,0:T(8,128)(2,1)}, u32[]{:S(2)}) %copy-start) | copy-done | bytes 2097176
  1.6 0.0 copy-start.1
  1.6 1.5 %copy-done.1 = bf16[1,8,30,8,512]{4,3,2,1,0:T(8,128)(2,1)S(1)} copy-done((bf16[1,8,30,8,512]{4,3,2,1,0:T(8,128)(2,1)S(1)}, bf16[1,8,30,8,512]{4,3,2,1,0:T(8,128)(2,1)}, u32[]{:S(2)}) %copy-start.1) | copy-done | bytes 1966104
  3.1 0.0 copy-start.2
  3.1 0.7 copy-done.2
  3.8 0.0 copy-start.3
  3.8 80.9 %shard_map.46 = bf16[240,512]{1,0:T(8,128)(2,1)S(1)} custom-call(s32[1,30]{1,0:T(1,128)S(1)} %copy-done.2, bf16[4,2,240,512]{3,2,1,0:T(8,128)(2,1)S(1)} %bitcast.6, bf16[2,2,512,512]{3,2,1,0:T(8,128)(2,1)S(1)} %bitcast.5), custom_call_target="tpu_custom_call" | custom-call | tf_op jit(solution)/shard_map/pallas_call | solution.py:233
  84.7 0.0 copy-done.3
  84.7 0.8 convert_add_fusion
Async XLA Ops:
  0.0 1.6 %copy-start = (bf16[1,1,2,2,512,512]{5,4,3,2,1,0:T(8,128)(2,1)S(1)}, bf16[1,1,2,2,512,512]{5,4,3,2,1,0:T(8,128)(2,1)}, u32[]{:S(2)}) copy-start(bf16[1,1,2,2,512,512]{5,4,3,2,1,0:T(8,128)(2,1)} %param.7) | copy-start | bytes 6291460
  1.6 1.5 %copy-start.1 = (bf16[1,8,30,8,512]{4,3,2,1,0:T(8,128)(2,1)S(1)}, bf16[1,8,30,8,512]{4,3,2,1,0:T(8,128)(2,1)}, u32[]{:S(2)}) copy-start(bf16[1,8,30,8,512]{4,3,2,1,0:T(8,128)(2,1)} %param.4) | copy-start | bytes 5898244
  3.1 0.7 copy-start.2
  3.8 80.9 %copy-start.3 = (f32[1,30,8,512]{3,2,1,0:T(8,128)S(1)}, f32[1,30,8,512]{3,2,1,0:T(8,128)}, u32[]{:S(2)}) copy-start(f32[1,30,8,512]{3,2,1,0:T(8,128)} %param.5) | copy-start | bytes 1474564

commit v2 on v1

v2 whole, which is shorter than its diff:
```python
import functools

import jax
import jax.numpy as jnp
from jax import lax
from jax.experimental import pallas as pl
from jax.experimental.pallas import tpu as pltpu
from jax.sharding import PartitionSpec as P

EPSILON = 1e-06
BETA = 0.9
MESH = pl.DeviceIdType.MESH
F32 = jnp.float32
BF16 = jnp.bfloat16


def iota(shape, dim):
    return lax.broadcasted_iota(jnp.int32, shape, dim)


def kernel(
    nodes, count, rows, width, slots,
    own_hbm, part, fac, out,
    owners, mine, sib0, sib1, sib2, psum0, psum1, psum2, own0, own1, own2, xin0, xin1, xin2,
    grad0, grad1, grad2, pick_both, pick_one, pick_in, held, outa, ina, outb, inb,
    block, left, prec, out2, in2, picked,
    sib_send, sib_recv, x_send, x_recv, senda, recva, sendb, recvb, send2, recv2,
    part_sem, fac_sem, own_sem,
):
    rep = lax.axis_index("rep")
    me = lax.axis_index("fsdp")
    chip, core = rep // 2, lax.rem(rep, 2)
    chips = part.shape[0]
    quarter = width // 4
    cols = width // 2
    lines = count * rows
    whole = nodes * rows
    sibling = {"rep": chip * 2 + 1 - core}
    spans = ((0, quarter), (quarter, quarter), (cols, cols))
    sib, psum, own = (sib0, sib1, sib2), (psum0, psum1, psum2), (own0, own1, own2)
    xin, grad = (xin0, xin1, xin2), (grad0, grad1, grad2)

    def fetch(i):
        side = pl.ds(*spans[i])
        return pltpu.make_async_copy(
            part.at[:, core, :, side], mine.at[:, :, side], part_sem.at[i]
        )

    for i in range(3):
        fetch(i).start()
    ids = pltpu.make_async_copy(own_hbm, owners, own_sem)
    ids.start()

    barrier = pltpu.get_barrier_semaphore()
    pl.semaphore_signal(barrier, inc=1, device_id=sibling, device_id_type=MESH)
    for k in range(1, chips):
        pl.semaphore_signal(
            barrier, inc=1, device_id={"rep": lax.rem(chip + k, chips) * 2 + core},
            device_id_type=MESH,
        )

    def greet(k, carry):
        pl.semaphore_signal(
            barrier, inc=1, device_id={"fsdp": lax.rem(me + k, nodes)}, device_id_type=MESH
        )
        return carry

    lax.fori_loop(1, nodes, greet, 0)
    pl.semaphore_wait(barrier, 1 + chips - 1 + nodes - 1)

    def to_sibling(i):
        return pltpu.make_async_remote_copy(
            src_ref=part.at[:, 1 - core, :, pl.ds(*spans[i])],
            dst_ref=sib[i],
            send_sem=sib_send.at[i],
            recv_sem=sib_recv.at[i],
            device_id=sibling,
            device_id_type=MESH,
        )

    for i in range(3):
        to_sibling(i).start()
    load = pltpu.make_async_copy(fac, held, fac_sem)
    load.start()

    def to_chip(i, k):
        return pltpu.make_async_remote_copy(
            src_ref=psum[i].at[k - 1],
            dst_ref=xin[i].at[k - 1],
            send_sem=x_send.at[i],
            recv_sem=x_recv.at[i],
            device_id={"rep": lax.rem(chip + k, chips) * 2 + core},
            device_id_type=MESH,
        )

    def x_bulk(i):
        return pltpu.make_async_remote_copy(
            src_ref=psum[i], dst_ref=xin[i], send_sem=x_send.at[i], recv_sem=x_recv.at[i],
            device_id=sibling, device_id_type=MESH,
        )

    def pair_sums(i):
        side = pl.ds(*spans[i])
        to_sibling(i).wait_recv()
        fetch(i).wait()
        for k in (2, 1, 3):
            other = lax.rem(chip + k, chips)
            pair = mine[other, :, side].astype(F32) + sib[i][other].astype(F32)
            psum[i][k - 1] = pair.astype(BF16)
            to_chip(i, k).start()
        own[i][...] = mine[chip, :, side].astype(F32) + sib[i][chip].astype(F32)

    def total(i):
        x_bulk(i).wait_recv()
        if i + 1 < 3:
            pair_sums(i + 1)
        acc = own[i][...]
        for k in range(chips - 1):
            acc = acc + xin[i][k].astype(F32)
        grad[i][...] = acc.astype(BF16)

    def send_loop(source, target, send, recv):
        def one(k, carry):
            p = lax.rem(me + k, nodes)
            pltpu.make_async_remote_copy(
                src_ref=source.at[p],
                dst_ref=target.at[me],
                send_sem=send,
                recv_sem=recv,
                device_id={"fsdp": p},
                device_id_type=MESH,
            ).start()
            return carry

        lax.fori_loop(1, nodes, one, 0)

    def bulk(source, target, send, recv):
        most = pl.ds(0, nodes - 1)
        return pltpu.make_async_remote_copy(
            src_ref=source.at[most],
            dst_ref=target.at[most],
            send_sem=send,
            recv_sem=recv,
            device_id={"fsdp": lax.rem(me + 1, nodes)},
            device_id_type=MESH,
        )

    ids.wait()
    lane_block = iota((32, lines), 1) // rows
    sub = iota((32, lines), 0)

    def spread(b, carry):
        lanes, subs = carry
        o = owners[0, b]
        return jnp.where(lane_block == b, o, lanes), jnp.where(sub == b, o, subs)

    own_lane, own_sub = lax.fori_loop(
        0, count, spread, (jnp.zeros((32, lines), jnp.int32), jnp.full((32, lines), -1, jnp.int32))
    )
    earlier = (own_lane == own_sub) & (sub < lane_block)
    slot_lane = jnp.sum(earlier.astype(jnp.int32), axis=0, keepdims=True)
    row_lane = lax.rem(iota((1, lines), 1), rows)
    place = (own_lane[0:1] * slots + slot_lane) * rows + row_lane
    step = 2 * rows * 4

    pair_sums(0)

    def build(i, carry):
        first = pl.multiple_of(i * step, step)
        match = iota((step, lines), 0) + first == place
        pick_both[pl.ds(first, step), :] = jnp.where(match, 1.0, 0.0).astype(BF16)
        return carry

    lax.fori_loop(0, slots * whole // step, build, 0)
    place_one = own_lane[0:1] * rows + row_lane
    for s in range(slots):
        here = jnp.where(slot_lane == s, place_one, -1)

        def build_one(i, carry, s=s, here=here):
            first = pl.multiple_of(i * step, step)
            match = iota((step, lines), 0) + first == here
            pick_one[s, pl.ds(first, step), :] = jnp.where(match, 1.0, 0.0).astype(BF16)
            return carry

        lax.fori_loop(0, whole // step, build_one, 0)

    for i in range(2):
        total(i)
        outa[i] = jnp.dot(pick_both[...], grad[i][...], preferred_element_type=F32).reshape(
            nodes, slots * rows, quarter
        ).astype(BF16)
        ina[i, me] = outa[i, me]
        send_loop(outa.at[i], ina.at[i], senda.at[i], recva.at[i])
    total(2)
    for s in range(slots):
        picked[...] = jnp.dot(pick_one[s], grad[2][...], preferred_element_type=F32)
        one = picked[:, :quarter].reshape(nodes, rows, quarter)
        two = picked[:, quarter:].reshape(nodes, rows, quarter)
        outb[s] = jnp.concatenate([one, two], axis=1).astype(BF16)
        inb[s, me] = outb[s, me]
        send_loop(outb.at[s], inb.at[s], sendb.at[s], recvb.at[s])

    row_block = iota((lines, 128), 0) // rows
    lane = iota((lines, 128), 1)

    def spread_rows(b, carry):
        mine_rows, others = carry
        o = owners[0, b]
        return jnp.where(row_block == b, o, mine_rows), jnp.where(lane == b, o, others)

    own_row, own_other = lax.fori_loop(
        0, count, spread_rows,
        (jnp.zeros((lines, 128), jnp.int32), jnp.full((lines, 128), -1, jnp.int32)),
    )
    earlier = (own_row == own_other) & (lane < row_block)
    slot_row = jnp.sum(earlier.astype(jnp.int32), axis=1, keepdims=True)
    place_row = own_row[:, 0:1] * rows + lax.rem(iota((lines, 1), 0), rows)
    for s in range(slots):
        here = jnp.where(slot_row == s, place_row, -1)
        match = iota((lines, whole), 1) == here
        pick_in[s] = jnp.where(match, 1.0, 0.0).astype(BF16)
    load.wait()

    squares = [jnp.zeros((rows, quarter), F32) for _ in range(slots)]
    for i in range(2):
        bulk(outa.at[i], ina.at[i], senda.at[i], recva.at[i]).wait_recv()
        for s in range(slots):
            wide = ina[i][:, s * rows : (s + 1) * rows].astype(F32)
            squares[s] = squares[s] + jnp.sum(wide * wide, axis=0)
            block[s, :, i * quarter : (i + 1) * quarter] = wide.reshape(whole, quarter).astype(BF16)
    for s in range(slots):
        left[s, :, :cols] = jnp.dot(
            held[s, 0], block[s, :, :cols], preferred_element_type=F32
        ).astype(BF16)
    for s in range(slots):
        bulk(outb.at[s], inb.at[s], sendb.at[s], recvb.at[s]).wait_recv()
        for q in range(2):
            wide = inb[s][:, q * rows : (q + 1) * rows].astype(F32)
            squares[s] = squares[s] + jnp.sum(wide * wide, axis=0)
            block[s, :, cols + q * quarter : cols + (q + 1) * quarter] = wide.reshape(
                whole, quarter
            ).astype(BF16)
        left[s, :, cols:] = jnp.dot(
            held[s, 0], block[s, :, cols:], preferred_element_type=F32
        ).astype(BF16)
        prec[...] = jnp.dot(left[s], held[s, 1], preferred_element_type=F32)
        prec_sq = jnp.sum(prec[...] * prec[...], keepdims=True).reshape(1, 1)
        grad_sq = jnp.sum(squares[s], keepdims=True).reshape(1, 1)
        ratio = jnp.sqrt(grad_sq / (prec_sq + EPSILON))
        update = prec[...] * ratio
        one = update[:, :cols].reshape(nodes, rows, cols)
        two = update[:, cols:].reshape(nodes, rows, cols)
        out2[s] = jnp.concatenate([one, two], axis=1).astype(BF16)
        in2[s, me] = out2[s, me]
        send_loop(out2.at[s], in2.at[s], send2.at[s], recv2.at[s])

    for s in range(slots):
        bulk(out2.at[s], in2.at[s], send2.at[s], recv2.at[s]).wait_recv()
        for h in range(2):
            rows_h = in2[s][:, h * rows : (h + 1) * rows].astype(F32).reshape(whole, cols)
            got = jnp.dot(pick_in[s], rows_h.astype(BF16), preferred_element_type=F32)
            if s == 0:
                prec[h * lines : (h + 1) * lines, :cols] = got
            else:
                got = got + prec[h * lines : (h + 1) * lines, :cols]
                out[:, h * cols : (h + 1) * cols] = got.astype(BF16)

    for i in range(3):
        to_sibling(i).wait_send()
        x_bulk(i).wait_send()
    for s in range(2):
        bulk(outa.at[s], ina.at[s], senda.at[s], recva.at[s]).wait_send()
        bulk(outb.at[s], inb.at[s], sendb.at[s], recvb.at[s]).wait_send()
        bulk(out2.at[s], in2.at[s], send2.at[s], recv2.at[s]).wait_send()


def local(partials, momentum, owners, factors):
    nodes = lax.axis_size("fsdp")
    slots = factors.shape[2]
    groups, count, rows, width = partials.shape[1:]
    lines = count * rows
    chips = groups // 2
    cols, quarter = width // 2, width // 4
    whole = nodes * rows
    widths = (quarter, quarter, cols)
    vmem, dma = pltpu.VMEM, pltpu.SemaphoreType.DMA
    update = pl.pallas_call(
        functools.partial(kernel, nodes, count, rows, width, slots),
        out_shape=jax.ShapeDtypeStruct((lines, width), BF16),
        in_specs=[
            pl.BlockSpec(memory_space=pltpu.HBM),
            pl.BlockSpec(memory_space=pltpu.HBM),
            pl.BlockSpec(memory_space=pltpu.HBM),
        ],
        out_specs=pl.BlockSpec(memory_space=pltpu.VMEM),
        scratch_shapes=[
            pltpu.SMEM((1, count), jnp.int32),
            vmem((chips, lines, width), BF16),
            *[vmem((chips, lines, w), BF16) for w in widths],
            *[vmem((chips - 1, lines, w), BF16) for w in widths],
            *[vmem((lines, w), F32) for w in widths],
            *[vmem((chips - 1, lines, w), BF16) for w in widths],
            *[vmem((lines, w), BF16) for w in widths],
            vmem((slots * whole, lines), BF16),
            vmem((slots, whole, lines), BF16),
            vmem((slots, lines, whole), BF16),
            vmem((slots, 2, width, width), BF16),
            vmem((2, nodes, slots * rows, quarter), BF16),
            vmem((2, nodes, slots * rows, quarter), BF16),
            vmem((slots, nodes, 2 * rows, quarter), BF16),
            vmem((slots, nodes, 2 * rows, quarter), BF16),
            vmem((slots, width, width), BF16),
            vmem((slots, width, width), BF16),
            vmem((width, width), F32),
            vmem((slots, nodes, 2 * rows, cols), BF16),
            vmem((slots, nodes, 2 * rows, cols), BF16),
            vmem((whole, cols), F32),
            dma((3,)), dma((3,)), dma((3,)), dma((3,)),
            dma((2,)), dma((2,)), dma((slots,)), dma((slots,)), dma((slots,)), dma((slots,)),
            dma((3,)), dma, dma,
        ],
        compiler_params=pltpu.CompilerParams(
            collective_id=0, has_side_effects=True, vmem_limit_bytes=60 << 20
        ),
    )(owners, partials.reshape(chips, 2, lines, width), factors[0, 0])
    return BETA * momentum + update.astype(F32).reshape(momentum.shape)


def solution(mesh):
    placed = (
        P("rep", None, None, "fsdp", None),
        P("rep", None, "fsdp", None),
        P("rep", None),
        P("rep", "fsdp", None, None, None, None),
    )
    return jax.shard_map(
        local, mesh=mesh, in_specs=placed, out_specs=P("rep", None, "fsdp", None), check_vma=False
    )
```

time: 85.7 us -> 77.7 us (0.907)
  Pallas kernels: 80.9 us -> 75.7 us
  local copies, waits for them, and re-layouts: 3.79 us -> 0.01 us
  other arithmetic: 0.85 us -> 1.79 us
    pallas_call x1, Pallas kernels: 80.9 us -> 75.7 us  [local(): pl.pallas_call(functools.partial(kernel, nodes, count, rows, width, slots...]
    unnamed x8 -> x2, local copies, waits for them, and re-layouts: 3.79 us -> 0.01 us
    add x1, other arithmetic: 0.85 us -> 1.79 us  [local(): return BETA * momentum + update.astype(F32).reshape(momentum.shape)]
where the time goes in v2:
time: 77.7 us; the launch traced here: 77.5 us
  Pallas kernels  75.7 us (97%)
  other arithmetic  1.79 us (2%)
    pallas_call x1, Pallas kernels, local(): pl.pallas_call(functools.partial(kernel, nodes, count, rows, width, slots...  75.7 us
    add x1, other arithmetic, local(): return BETA * momentum + update.astype(F32).reshape(momentum.shape)  1.79 us

profile of v2, /device:TPU:1, one launch (start us, length us, event | category | flops | bytes accessed | tf_op | source)
XLA Modules:
  0.0 77.5 jit_solution(13024735727900052339)
XLA Ops:
  0.0 0.0 copy-start
  0.0 75.7 %shard_map.46 = bf16[240,512]{1,0:T(8,128)(2,1)} custom-call(s32[1,30]{1,0:T(1,128)} %own_hbm.1, bf16[4,2,240,512]{3,2,1,0:T(8,128)(2,1)} %bitcast.6, bf16[2,2,512,512]{3,2,1,0:T(8,128)(2,1)} %bitcast.5), custom_call_target="tpu_custom_call" | custom-call | tf_op jit(solution)/shard_map/pallas_call | solution.py:287
  75.7 0.0 copy-done
  75.7 1.8 %convert_add_fusion = f32[1,30,8,512]{3,2,1,0:T(8,128)} fusion(f32[1,30,8,512]{3,2,1,0:T(8,128)S(1)} %copy-done, bf16[240,512]{1,0:T(8,128)(2,1)} %shard_map.46), kind=kLoop, calls=%fused_computation | loop fusion | flops 368640 | bytes 1228800 | tf_op jit(solution)/shard_map/add | solution.py:326
Async XLA Ops:
  0.0 75.7 %copy-start = (f32[1,30,8,512]{3,2,1,0:T(8,128)S(1)}, f32[1,30,8,512]{3,2,1,0:T(8,128)}, u32[]{:S(2)}) copy-start(f32[1,30,8,512]{3,2,1,0:T(8,128)} %param.5) | copy-start | bytes 1474564

commit v3 on v2

--- a/solution.py
+++ b/solution.py
@@ -25,12 +25,13 @@
     grad0, grad1, grad2, pick_both, pick_one, pick_in, held, outa, ina, outb, inb,
     block, left, prec, out2, in2, picked,
     sib_send, sib_recv, x_send, x_recv, senda, recva, sendb, recvb, send2, recv2,
-    part_sem, fac_sem, own_sem,
+    part_sem, fac_sem, own_sem, line_sem,
 ):
     rep = lax.axis_index("rep")
     me = lax.axis_index("fsdp")
     chip, core = rep // 2, lax.rem(rep, 2)
     chips = part.shape[0]
+    side = 8
     quarter = width // 4
     cols = width // 2
     lines = count * rows
@@ -41,9 +42,9 @@
     xin, grad = (xin0, xin1, xin2), (grad0, grad1, grad2)
 
     def fetch(i):
-        side = pl.ds(*spans[i])
+        span = pl.ds(*spans[i])
         return pltpu.make_async_copy(
-            part.at[:, core, :, side], mine.at[:, :, side], part_sem.at[i]
+            part.at[:, core, :, span], mine.at[:, :, span], part_sem.at[i]
         )
 
     for i in range(3):
@@ -59,14 +60,20 @@
             device_id_type=MESH,
         )
 
-    def greet(k, carry):
-        pl.semaphore_signal(
-            barrier, inc=1, device_id={"fsdp": lax.rem(me + k, nodes)}, device_id_type=MESH
-        )
-        return carry
-
-    lax.fori_loop(1, nodes, greet, 0)
-    pl.semaphore_wait(barrier, 1 + chips - 1 + nodes - 1)
+    y, z = me // side, lax.rem(me, side)
+
+    def along_y(k):
+        return lax.rem(y + k, side) * side + z
+
+    def along_z(k):
+        return y * side + lax.rem(z + k, side)
+
+    for k in range(1, side):
+        for peer in (along_z(k), along_y(k)):
+            pl.semaphore_signal(
+                barrier, inc=1, device_id={"fsdp": peer}, device_id_type=MESH
+            )
+    pl.semaphore_wait(barrier, 1 + chips - 1 + 2 * (side - 1))
 
     def to_sibling(i):
         return pltpu.make_async_remote_copy(
@@ -80,6 +87,10 @@
 
     for i in range(3):
         to_sibling(i).start()
+    for k in range(1, side):
+        pl.semaphore_signal(
+            line_sem, inc=1, device_id={"fsdp": along_y(k)}, device_id_type=MESH
+        )
     load = pltpu.make_async_copy(fac, held, fac_sem)
     load.start()
 
@@ -100,15 +111,15 @@
         )
 
     def pair_sums(i):
-        side = pl.ds(*spans[i])
+        span = pl.ds(*spans[i])
         to_sibling(i).wait_recv()
         fetch(i).wait()
         for k in (2, 1, 3):
             other = lax.rem(chip + k, chips)
-            pair = mine[other, :, side].astype(F32) + sib[i][other].astype(F32)
+            pair = mine[other, :, span].astype(F32) + sib[i][other].astype(F32)
             psum[i][k - 1] = pair.astype(BF16)
             to_chip(i, k).start()
-        own[i][...] = mine[chip, :, side].astype(F32) + sib[i][chip].astype(F32)
+        own[i][...] = mine[chip, :, span].astype(F32) + sib[i][chip].astype(F32)
 
     def total(i):
         x_bulk(i).wait_recv()
@@ -183,6 +194,8 @@
             return carry
 
         lax.fori_loop(0, whole // step, build_one, 0)
+
+    pl.semaphore_wait(line_sem, side - 1)
 
     for i in range(2):
         total(i)
@@ -317,7 +330,7 @@
             vmem((whole, cols), F32),
             dma((3,)), dma((3,)), dma((3,)), dma((3,)),
             dma((2,)), dma((2,)), dma((slots,)), dma((slots,)), dma((slots,)), dma((slots,)),
-            dma((3,)), dma, dma,
+            dma((3,)), dma, dma, pltpu.SemaphoreType.REGULAR,
         ],
         compiler_params=pltpu.CompilerParams(
             collective_id=0, has_side_effects=True, vmem_limit_bytes=60 << 20

time: 77.7 us -> 75.2 us (0.968)
  Pallas kernels: 75.7 us -> 73.2 us
    pallas_call x1, Pallas kernels: 75.7 us -> 73.2 us  [local(): pl.pallas_call(functools.partial(kernel, nodes, count, rows, width, slots...]
where the time goes in v3:
time: 75.2 us; the launch traced here: 75.1 us
  Pallas kernels  73.2 us (97%)
  other arithmetic  1.79 us (2%)
    pallas_call x1, Pallas kernels, local(): pl.pallas_call(functools.partial(kernel, nodes, count, rows, width, slots...  73.2 us
    add x1, other arithmetic, local(): return BETA * momentum + update.astype(F32).reshape(momentum.shape)  1.79 us

profile of v3, /device:TPU:1, one launch (start us, length us, event | category | flops | bytes accessed | tf_op | source)
XLA Modules:
  0.0 75.1 jit_solution(11006873769279775198)
XLA Ops:
  0.0 0.0 copy-start
  0.0 73.2 %shard_map.46 = bf16[240,512]{1,0:T(8,128)(2,1)} custom-call(s32[1,30]{1,0:T(1,128)} %own_hbm.1, bf16[4,2,240,512]{3,2,1,0:T(8,128)(2,1)} %bitcast.6, bf16[2,2,512,512]{3,2,1,0:T(8,128)(2,1)} %bitcast.5), custom_call_target="tpu_custom_call" | custom-call | tf_op jit(solution)/shard_map/pallas_call | solution.py:300
  73.3 0.0 copy-done
  73.3 1.8 %convert_add_fusion = f32[1,30,8,512]{3,2,1,0:T(8,128)} fusion(f32[1,30,8,512]{3,2,1,0:T(8,128)S(1)} %copy-done, bf16[240,512]{1,0:T(8,128)(2,1)} %shard_map.46), kind=kLoop, calls=%fused_computation | loop fusion | flops 368640 | bytes 1228800 | tf_op jit(solution)/shard_map/add | solution.py:339
Async XLA Ops:
  0.0 73.3 %copy-start = (f32[1,30,8,512]{3,2,1,0:T(8,128)S(1)}, f32[1,30,8,512]{3,2,1,0:T(8,128)}, u32[]{:S(2)}) copy-start(f32[1,30,8,512]{3,2,1,0:T(8,128)} %param.5) | copy-start | bytes 1474564

commit v4 on v3

--- a/solution.py
+++ b/solution.py
@@ -25,7 +25,7 @@
     grad0, grad1, grad2, pick_both, pick_one, pick_in, held, outa, ina, outb, inb,
     block, left, prec, out2, in2, picked,
     sib_send, sib_recv, x_send, x_recv, senda, recva, sendb, recvb, send2, recv2,
-    part_sem, fac_sem, own_sem, line_sem,
+    part_sem, fac_sem, own_sem, after_sem, line_sem,
 ):
     rep = lax.axis_index("rep")
     me = lax.axis_index("fsdp")
@@ -47,8 +47,7 @@
             part.at[:, core, :, span], mine.at[:, :, span], part_sem.at[i]
         )
 
-    for i in range(3):
-        fetch(i).start()
+    fetch(0).start()
     ids = pltpu.make_async_copy(own_hbm, owners, own_sem)
     ids.start()
 
@@ -62,18 +61,26 @@
 
     y, z = me // side, lax.rem(me, side)
 
-    def along_y(k):
-        return lax.rem(y + k, side) * side + z
-
-    def along_z(k):
-        return y * side + lax.rem(z + k, side)
-
-    for k in range(1, side):
-        for peer in (along_z(k), along_y(k)):
-            pl.semaphore_signal(
-                barrier, inc=1, device_id={"fsdp": peer}, device_id_type=MESH
-            )
-    pl.semaphore_wait(barrier, 1 + chips - 1 + 2 * (side - 1))
+    def peer(at_y, at_z):
+        return {"fsdp": at_y * side + at_z}
+
+    half = side // 2
+    turn = jnp.where(y < half, y, side + half - 1 - y)
+
+    def at_turn(j):
+        return jnp.where(j < half, j, side + half - 1 - j)
+
+    def tell(semaphore, first, last, along_y):
+        def one(j, carry):
+            to = peer(at_turn(j), z) if along_y else peer(y, j)
+            pl.semaphore_signal(semaphore, inc=1, device_id=to, device_id_type=MESH)
+            return carry
+
+        lax.fori_loop(first, last, one, 0)
+
+    tell(barrier, z + 1, side, False)
+    tell(barrier, turn + 1, side, True)
+    pl.semaphore_wait(barrier, 1 + chips - 1 + turn + z)
 
     def to_sibling(i):
         return pltpu.make_async_remote_copy(
@@ -87,12 +94,11 @@
 
     for i in range(3):
         to_sibling(i).start()
-    for k in range(1, side):
-        pl.semaphore_signal(
-            line_sem, inc=1, device_id={"fsdp": along_y(k)}, device_id_type=MESH
-        )
+    for i in range(1, 3):
+        fetch(i).start()
+    tell(after_sem, 0, z, False)
+    tell(after_sem, 0, turn, True)
     load = pltpu.make_async_copy(fac, held, fac_sem)
-    load.start()
 
     def to_chip(i, k):
         return pltpu.make_async_remote_copy(
@@ -118,13 +124,15 @@
             other = lax.rem(chip + k, chips)
             pair = mine[other, :, span].astype(F32) + sib[i][other].astype(F32)
             psum[i][k - 1] = pair.astype(BF16)
-            to_chip(i, k).start()
+            if i == 0:
+                to_chip(i, k).start()
         own[i][...] = mine[chip, :, span].astype(F32) + sib[i][chip].astype(F32)
 
     def total(i):
         x_bulk(i).wait_recv()
         if i + 1 < 3:
-            pair_sums(i + 1)
+            for k in (2, 1, 3):
+                to_chip(i + 1, k).start()
         acc = own[i][...]
         for k in range(chips - 1):
             acc = acc + xin[i][k].astype(F32)
@@ -132,7 +140,7 @@
 
     def send_loop(source, target, send, recv):
         def one(k, carry):
-            p = lax.rem(me + k, nodes)
+            p = lax.rem(me + k * 27, nodes)
             pltpu.make_async_remote_copy(
                 src_ref=source.at[p],
                 dst_ref=target.at[me],
@@ -175,6 +183,7 @@
     step = 2 * rows * 4
 
     pair_sums(0)
+    load.start()
 
     def build(i, carry):
         first = pl.multiple_of(i * step, step)
@@ -183,18 +192,16 @@
         return carry
 
     lax.fori_loop(0, slots * whole // step, build, 0)
-    place_one = own_lane[0:1] * rows + row_lane
-    for s in range(slots):
-        here = jnp.where(slot_lane == s, place_one, -1)
-
-        def build_one(i, carry, s=s, here=here):
-            first = pl.multiple_of(i * step, step)
-            match = iota((step, lines), 0) + first == here
-            pick_one[s, pl.ds(first, step), :] = jnp.where(match, 1.0, 0.0).astype(BF16)
-            return carry
-
-        lax.fori_loop(0, whole // step, build_one, 0)
-
+    pair_sums(1)
+
+    later = 2 * (side - 1) - turn - z
+
+    @pl.when(later > 0)
+    def _():
+        pl.semaphore_wait(after_sem, later)
+
+    tell(line_sem, 0, turn, True)
+    tell(line_sem, turn + 1, side, True)
     pl.semaphore_wait(line_sem, side - 1)
 
     for i in range(2):
@@ -204,6 +211,21 @@
         ).astype(BF16)
         ina[i, me] = outa[i, me]
         send_loop(outa.at[i], ina.at[i], senda.at[i], recva.at[i])
+        if i == 0:
+            pair_sums(2)
+
+    place_one = own_lane[0:1] * rows + row_lane
+    for s in range(slots):
+        here = jnp.where(slot_lane == s, place_one, -1)
+
+        def build_one(i, carry, s=s, here=here):
+            first = pl.multiple_of(i * step, step)
+            match = iota((step, lines), 0) + first == here
+            pick_one[s, pl.ds(first, step), :] = jnp.where(match, 1.0, 0.0).astype(BF16)
+            return carry
+
+        lax.fori_loop(0, whole // step, build_one, 0)
+
     total(2)
     for s in range(slots):
         picked[...] = jnp.dot(pick_one[s], grad[2][...], preferred_element_type=F32)
@@ -330,10 +352,11 @@
             vmem((whole, cols), F32),
             dma((3,)), dma((3,)), dma((3,)), dma((3,)),
             dma((2,)), dma((2,)), dma((slots,)), dma((slots,)), dma((slots,)), dma((slots,)),
-            dma((3,)), dma, dma, pltpu.SemaphoreType.REGULAR,
+            dma((3,)), dma, dma,
+            pltpu.SemaphoreType.REGULAR, pltpu.SemaphoreType.REGULAR,
         ],
         compiler_params=pltpu.CompilerParams(
-            collective_id=0, has_side_effects=True, vmem_limit_bytes=60 << 20
+            collective_id=0, has_side_effects=True, vmem_limit_bytes=53 << 20
         ),
     )(owners, partials.reshape(chips, 2, lines, width), factors[0, 0])
     return BETA * momentum + update.astype(F32).reshape(momentum.shape)

time: 75.2 us -> 72.8 us (0.968)
  Pallas kernels: 73.2 us -> 71.1 us
  other arithmetic: 1.79 us -> 0.85 us
    pallas_call x1, Pallas kernels: 73.2 us -> 71.1 us  [local(): pl.pallas_call(functools.partial(kernel, nodes, count, rows, width, slots...]
    add x1, other arithmetic: 1.79 us -> 0.85 us  [local(): return BETA * momentum + update.astype(F32).reshape(momentum.shape)]
where the time goes in v4:
time: 72.8 us; the launch traced here: 72.7 us
  Pallas kernels  71.1 us (98%)
  other arithmetic  0.85 us (1%)
    pallas_call x1, Pallas kernels, local(): pl.pallas_call(functools.partial(kernel, nodes, count, rows, width, slots...  71.1 us

profile of v4, /device:TPU:1, one launch (start us, length us, event | category | flops | bytes accessed | tf_op | source)
XLA Modules:
  0.0 72.7 jit_solution(1824758555843187620)
XLA Ops:
  0.0 0.0 copy-start
  0.0 0.7 copy-done
  0.7 0.0 copy-start.1
  0.7 71.1 %shard_map.46 = bf16[240,512]{1,0:T(8,128)(2,1)S(1)} custom-call(s32[1,30]{1,0:T(1,128)S(1)} %copy-done, bf16[4,2,240,512]{3,2,1,0:T(8,128)(2,1)} %bitcast.6, bf16[2,2,512,512]{3,2,1,0:T(8,128)(2,1)} %bitcast.5), custom_call_target="tpu_custom_call" | custom-call | tf_op jit(solution)/shard_map/pallas_call | solution.py:322
  71.8 0.0 copy-done.1
  71.8 0.8 %convert_add_fusion = f32[1,30,8,512]{3,2,1,0:T(8,128)} fusion(f32[1,30,8,512]{3,2,1,0:T(8,128)S(1)} %copy-done.1, bf16[240,512]{1,0:T(8,128)(2,1)S(1)} %shard_map.46), kind=kLoop, calls=%fused_computation | loop fusion | flops 368640 | bytes 1228800 | tf_op jit(solution)/shard_map/add | solution.py:362
Async XLA Ops:
  0.0 0.7 copy-start
  0.7 71.2 %copy-start.1 = (f32[1,30,8,512]{3,2,1,0:T(8,128)S(1)}, f32[1,30,8,512]{3,2,1,0:T(8,128)}, u32[]{:S(2)}) copy-start(f32[1,30,8,512]{3,2,1,0:T(8,128)} %param.5) | copy-start | bytes 1474564

commit v5 on v4

--- a/solution.py
+++ b/solution.py
@@ -140,7 +140,8 @@
 
     def send_loop(source, target, send, recv):
         def one(k, carry):
-            p = lax.rem(me + k * 27, nodes)
+            o = lax.rem(k * 27, nodes)
+            p = lax.rem(y + o // side, side) * side + lax.rem(z + o, side)
             pltpu.make_async_remote_copy(
                 src_ref=source.at[p],
                 dst_ref=target.at[me],

time: 72.8 us -> 72.4 us (level); the launches traced: 72.7 us -> 71.5 us
  Pallas kernels: 71.1 us -> 70 us
    pallas_call x1, Pallas kernels: 71.1 us -> 70 us  [local(): pl.pallas_call(functools.partial(kernel, nodes, count, rows, width, slots...]
where the time goes in v5:
time: 72.4 us; the launch traced here: 71.5 us
  Pallas kernels  70 us (97%)
  other arithmetic  0.85 us (1%)
    pallas_call x1, Pallas kernels, local(): pl.pallas_call(functools.partial(kernel, nodes, count, rows, width, slots...  70 us

profile of v5, /device:TPU:1, one launch (start us, length us, event | category | flops | bytes accessed | tf_op | source)
XLA Modules:
  0.0 71.5 jit_solution(5639788637632583539)
XLA Ops:
  0.0 0.0 copy-start
  0.0 0.7 copy-done
  0.7 0.0 copy-start.1
  0.7 70.0 %shard_map.46 = bf16[240,512]{1,0:T(8,128)(2,1)S(1)} custom-call(s32[1,30]{1,0:T(1,128)S(1)} %copy-done, bf16[4,2,240,512]{3,2,1,0:T(8,128)(2,1)} %bitcast.6, bf16[2,2,512,512]{3,2,1,0:T(8,128)(2,1)} %bitcast.5), custom_call_target="tpu_custom_call" | custom-call | tf_op jit(solution)/shard_map/pallas_call | solution.py:323
  70.7 0.0 copy-done.1
  70.7 0.8 %convert_add_fusion = f32[1,30,8,512]{3,2,1,0:T(8,128)} fusion(f32[1,30,8,512]{3,2,1,0:T(8,128)S(1)} %copy-done.1, bf16[240,512]{1,0:T(8,128)(2,1)S(1)} %shard_map.46), kind=kLoop, calls=%fused_computation | loop fusion | flops 368640 | bytes 1228800 | tf_op jit(solution)/shard_map/add | solution.py:363
Async XLA Ops:
  0.0 0.7 copy-start
  0.7 70.0 %copy-start.1 = (f32[1,30,8,512]{3,2,1,0:T(8,128)S(1)}, f32[1,30,8,512]{3,2,1,0:T(8,128)}, u32[]{:S(2)}) copy-start(f32[1,30,8,512]{3,2,1,0:T(8,128)} %param.5) | copy-start | bytes 1474564

commit v6 on v5

--- a/solution.py
+++ b/solution.py
@@ -165,6 +165,9 @@
             device_id_type=MESH,
         )
 
+    pair_sums(0)
+    load.start()
+
     ids.wait()
     lane_block = iota((32, lines), 1) // rows
     sub = iota((32, lines), 0)
@@ -182,9 +185,6 @@
     row_lane = lax.rem(iota((1, lines), 1), rows)
     place = (own_lane[0:1] * slots + slot_lane) * rows + row_lane
     step = 2 * rows * 4
-
-    pair_sums(0)
-    load.start()
 
     def build(i, carry):
         first = pl.multiple_of(i * step, step)

time: 72.4 us -> 72.4 us (level)
  no operation moved by 1% of the time
where the time goes in v6:
time: 72.4 us; the launch traced here: 71.5 us
  Pallas kernels  70 us (97%)
  other arithmetic  0.85 us (1%)
    pallas_call x1, Pallas kernels, local(): pl.pallas_call(functools.partial(kernel, nodes, count, rows, width, slots...  70 us

profile of v6, /device:TPU:1, one launch (start us, length us, event | category | flops | bytes accessed | tf_op | source)
XLA Modules:
  0.0 71.5 jit_solution(4895155210595873948)
XLA Ops:
  0.0 0.0 copy-start
  0.0 0.7 copy-done
  0.7 0.0 copy-start.1
  0.7 70.0 %shard_map.46 = bf16[240,512]{1,0:T(8,128)(2,1)S(1)} custom-call(s32[1,30]{1,0:T(1,128)S(1)} %copy-done, bf16[4,2,240,512]{3,2,1,0:T(8,128)(2,1)} %bitcast.6, bf16[2,2,512,512]{3,2,1,0:T(8,128)(2,1)} %bitcast.5), custom_call_target="tpu_custom_call" | custom-call | tf_op jit(solution)/shard_map/pallas_call | solution.py:323
  70.7 0.0 copy-done.1
  70.7 0.8 %convert_add_fusion = f32[1,30,8,512]{3,2,1,0:T(8,128)} fusion(f32[1,30,8,512]{3,2,1,0:T(8,128)S(1)} %copy-done.1, bf16[240,512]{1,0:T(8,128)(2,1)S(1)} %shard_map.46), kind=kLoop, calls=%fused_computation | loop fusion | flops 368640 | bytes 1228800 | tf_op jit(solution)/shard_map/add | solution.py:363
Async XLA Ops:
  0.0 0.7 copy-start
  0.7 70.0 %copy-start.1 = (f32[1,30,8,512]{3,2,1,0:T(8,128)S(1)}, f32[1,30,8,512]{3,2,1,0:T(8,128)}, u32[]{:S(2)}) copy-start(f32[1,30,8,512]{3,2,1,0:T(8,128)} %param.5) | copy-start | bytes 1474564
